TPU v7x, 512 devices: a whole 4x4x16 slice. The times are simulated.
512 devices in a mesh: ctx: 32 (over y, x, core), head: 16 (over z).
Axes of the slice: x: 4, y: 4, z: 16, core: 2. Of those that a mesh axis runs over, the one named last changes fastest.
Arguments:
- queries: bfloat16 [8192, 4096], P('ctx', 'head'), may hold values from -50 to 50
- keys: bfloat16 [8192, 4096], P('ctx', 'head'), may hold values from -9 to 9
- values: bfloat16 [8192, 4096], P('ctx', 'head'), may hold values from -9 to 9
- near_blocks: int32 [64, 4], P('ctx'), may hold values from 0 to 63, as said below
- near_count: int32 [64], P('ctx'), may hold values from 1 to 4
- head_scale: float32 [32], P('head'), may hold values from 0.2 to 4.2
- gain: float32 [4096], P('head'), may hold values from 0.5 to 1.5
- cotangent: bfloat16 [8192, 4096], P('ctx', 'head'), may hold values from -6 to 6
Outputs:
- mixed: bfloat16 [8192, 4096], P('ctx', 'head')
- grad_queries: bfloat16 [8192, 4096], P('ctx', 'head')
- grad_keys: bfloat16 [8192, 4096], P('ctx', 'head')
- grad_values: bfloat16 [8192, 4096], P('ctx', 'head')
Inputs may be any that keep to these rules, and one draw needn't show every extreme that they name: near_blocks[b, 0] = b; entries 1 to near_count[b] - 1 are distinct blocks other than b within 2 blocks of b; the later entries equal b.
All inputs are finite; a program needn't handle non-finite values.
Results may differ from a plain program's by a relative error of at most 0.022.
Values may be sent and summed in bfloat16 or wider, within the bound.
A program may use at most 64 MiB of HBM per device.

v0:
```python
import math
import jax
import jax.numpy as jnp
from jax import lax
from jax.sharding import PartitionSpec as P

HEADS = 32
HEAD_SIZE = 128
BLOCK_TOKENS = 128
NEAR_SLOTS = 4
RB = 2
LEV = 5
LOG_TWO = 0.6931471805599453
NEG_BIG = -1e30
NORM_EPS = 1e-05


def padded_2(cells, sides, width):
    for axis, dim in sides:
        count = lax.axis_size(axis)
        ends = count - 1
        head = lax.slice_in_dim(cells, 0, width, axis=dim)
        tail = lax.slice_in_dim(cells, cells.shape[dim] - width, cells.shape[dim], axis=dim)
        cells = jnp.concatenate(
            [
                lax.ppermute(tail, axis, [(i, (i + 1) % count) for i in range(ends)]),
                cells,
                lax.ppermute(head, axis, [((i + 1) % count, i) for i in range(ends)]),
            ],
            axis=dim,
        )
    return cells


def passed_along(value, axis, by):
    size = lax.axis_size(axis)
    pairs = [(i, i + by) for i in range(size) if 0 <= i + by < size]
    return lax.ppermute(value, axis, pairs)


def shortened(value):

    def short(part):
        return part.astype(jnp.bfloat16) if part.dtype == jnp.float32 else part

    return jax.tree.map(short, value)


def from_partner(value, axis, apart):
    mask = 2**apart
    pairs = [(source, source ^ mask) for source in range(lax.axis_size(axis))]
    return lax.ppermute(value, axis, pairs)


def body(queries, keys, values, near_blocks, near_count, head_scale, gain, cotangent):
    tok_rows = queries.shape[0]
    local_cols = queries.shape[1]
    heads_here = local_cols // HEAD_SIZE
    width = HEADS * HEAD_SIZE
    ctx_count = lax.axis_size("ctx")
    device = lax.axis_index("ctx")
    blocks_here = tok_rows // BLOCK_TOKENS
    margin = RB * BLOCK_TOKENS
    extended = blocks_here + 2 * RB
    columns = 2 * local_cols
    softmax_scale = 1.0 / math.sqrt(HEAD_SIZE)
    pair = jnp.concatenate([keys, values], axis=1)
    padded = padded_2(pair, (("ctx", 0),), margin)
    first_block = device * blocks_here - RB
    select = (near_blocks - first_block)[:, :, None] == jnp.arange(extended, dtype=jnp.int32)[
        None, None, :
    ]
    select_flat = select.reshape(blocks_here * NEAR_SLOTS, extended)
    near_pair = jnp.dot(
        select_flat.astype(jnp.bfloat16),
        padded.reshape(extended, BLOCK_TOKENS * columns),
        preferred_element_type=jnp.float32,
    )
    near_pair = near_pair.astype(jnp.bfloat16).reshape(
        blocks_here, NEAR_SLOTS, BLOCK_TOKENS, columns
    )
    valid = jnp.arange(NEAR_SLOTS, dtype=jnp.int32)[None, :] < near_count[:, None]
    key_mask = jnp.repeat(valid, BLOCK_TOKENS, axis=1)[:, None, :]
    factors = [2 ** (level_idx + 1) for level_idx in range(LEV)]
    groups = [min(2 ** (level_idx + 1), ctx_count) for level_idx in range(LEV)]
    pooled = [
        pair.astype(jnp.float32)
        .reshape(tok_rows // factors[level_idx], factors[level_idx], columns)
        .mean(axis=1)
        .astype(jnp.bfloat16)
        for level_idx in range(LEV)
    ]
    steps_count = max(groups).bit_length() - 1
    q_global = device * tok_rows + jnp.arange(tok_rows, dtype=jnp.int32)
    far_masks = []
    for level_idx in range(LEV):
        span_here = groups[level_idx] * tok_rows
        rows_level = span_here // factors[level_idx]
        group_first = device // groups[level_idx] * span_here
        key_first = group_first + jnp.arange(rows_level, dtype=jnp.int32) * factors[level_idx]
        keep = jnp.abs(key_first[None, :] // BLOCK_TOKENS - q_global[:, None] // BLOCK_TOKENS) > RB
        if level_idx > 0:
            prior = groups[level_idx - 1] * tok_rows
            keep = keep & (key_first[None, :] // prior != q_global[:, None] // prior)
        far_masks.append(keep)
    group_pair = list(pooled)
    shared = [level_idx for level_idx in range(LEV) if groups[level_idx] > 1]
    packed = jnp.concatenate([pooled[level_idx] for level_idx in shared], axis=0)
    everyone = lax.all_gather(packed, "ctx", axis=0, tiled=True).reshape(
        ctx_count, packed.shape[0], columns
    )
    offset = 0
    for level_idx in shared:
        count_rows = pooled[level_idx].shape[0]
        piece = everyone[:, offset : offset + count_rows]
        group_start = device // groups[level_idx] * groups[level_idx]
        chosen = lax.dynamic_slice_in_dim(piece, group_start, groups[level_idx], 0)
        group_pair[level_idx] = chosen.reshape(groups[level_idx] * count_rows, columns)
        offset = offset + count_rows
    saved = []
    attn_list = []
    for head_idx in range(heads_here):
        k_cols = slice(head_idx * HEAD_SIZE, (head_idx + 1) * HEAD_SIZE)
        v_cols = slice((heads_here + head_idx) * HEAD_SIZE, (heads_here + head_idx + 1) * HEAD_SIZE)
        q_head = queries[:, k_cols]
        query_blocks = q_head.reshape(blocks_here, BLOCK_TOKENS, HEAD_SIZE)
        near_key_rows = near_pair[:, :, :, k_cols].reshape(
            blocks_here, NEAR_SLOTS * BLOCK_TOKENS, HEAD_SIZE
        )
        near_value_rows = near_pair[:, :, :, v_cols].reshape(
            blocks_here, NEAR_SLOTS * BLOCK_TOKENS, HEAD_SIZE
        )
        near_score_rows = (
            jnp.einsum(
                "mne,mge->mng", query_blocks, near_key_rows, preferred_element_type=jnp.float32
            )
            * softmax_scale
        )
        near_score_rows = jnp.where(key_mask, near_score_rows, NEG_BIG)
        top = jnp.max(near_score_rows, axis=2).reshape(tok_rows)
        coarse_k = [group_pair[level_idx][:, k_cols] for level_idx in range(LEV)]
        coarse_v = [group_pair[level_idx][:, v_cols] for level_idx in range(LEV)]
        s_far = []
        for level_idx in range(LEV):
            scores = (
                jnp.einsum(
                    "td,kd->tk", q_head, coarse_k[level_idx], preferred_element_type=jnp.float32
                )
                * softmax_scale
                + (level_idx + 1) * LOG_TWO
            )
            scores = jnp.where(far_masks[level_idx], scores, NEG_BIG)
            s_far.append(scores)
            top = jnp.maximum(top, jnp.max(scores, axis=1))
        p_near = jnp.where(
            key_mask, jnp.exp(near_score_rows - top.reshape(blocks_here, BLOCK_TOKENS, 1)), 0.0
        )
        total = jnp.sum(p_near, axis=2).reshape(tok_rows)
        p_far = []
        for level_idx in range(LEV):
            exps = jnp.where(far_masks[level_idx], jnp.exp(s_far[level_idx] - top[:, None]), 0.0)
            p_far.append(exps)
            total = total + jnp.sum(exps, axis=1)
        prob_near = p_near / total.reshape(blocks_here, BLOCK_TOKENS, 1)
        near_weight_rows = prob_near.astype(jnp.bfloat16)
        attention_output = jnp.einsum(
            "itp,ipc->itc", near_weight_rows, near_value_rows, preferred_element_type=jnp.float32
        ).reshape(tok_rows, HEAD_SIZE)
        prob_far = []
        weight_far = []
        for level_idx in range(LEV):
            probs = p_far[level_idx] / total[:, None]
            weights_bf = probs.astype(jnp.bfloat16)
            prob_far.append(probs)
            weight_far.append(weights_bf)
            attention_output = attention_output + jnp.dot(
                weights_bf, coarse_v[level_idx], preferred_element_type=jnp.float32
            )
        attn_list.append(attention_output)
        saved.append(
            (
                q_head,
                query_blocks,
                near_key_rows,
                near_value_rows,
                prob_near,
                near_weight_rows,
                coarse_k,
                coarse_v,
                prob_far,
                weight_far,
            )
        )
    scaled = jnp.concatenate(
        [attn_list[head_idx] * head_scale[head_idx] for head_idx in range(heads_here)], axis=1
    )
    squares = lax.psum(jnp.sum(scaled * scaled, axis=1), "head")
    inv = lax.rsqrt(squares / width + NORM_EPS)
    mixed = (scaled * inv[:, None] * gain[None, :]).astype(jnp.bfloat16)
    back = cotangent.astype(jnp.float32) * gain[None, :]
    inner = lax.psum(jnp.sum(back * scaled, axis=1), "head")
    d_scaled = inv[:, None] * (back - scaled * (inv * inv * inner / width)[:, None])
    grad_q_list = []
    near_dk = []
    near_dv = []
    far_dk = [[] for level_idx in range(LEV)]
    far_dv = [[] for level_idx in range(LEV)]
    for head_idx in range(heads_here):
        (
            q_head,
            query_blocks,
            near_key_rows,
            near_value_rows,
            prob_near,
            near_weight_rows,
            coarse_k,
            coarse_v,
            prob_far,
            weight_far,
        ) = saved[head_idx]
        d_out = (
            d_scaled[:, head_idx * HEAD_SIZE : (head_idx + 1) * HEAD_SIZE] * head_scale[head_idx]
        ).astype(jnp.bfloat16)
        delta = jnp.sum(d_out.astype(jnp.float32) * attn_list[head_idx], axis=1)
        block_gradient = d_out.reshape(blocks_here, BLOCK_TOKENS, HEAD_SIZE)
        near_prob_gradient = jnp.einsum(
            "mne,mge->mng", block_gradient, near_value_rows, preferred_element_type=jnp.float32
        )
        near_score_gradient = (
            prob_near * (near_prob_gradient - delta.reshape(blocks_here, BLOCK_TOKENS, 1))
        ).astype(jnp.bfloat16)
        query_gradient = jnp.einsum(
            "itp,ipc->itc", near_score_gradient, near_key_rows, preferred_element_type=jnp.float32
        ).reshape(tok_rows, HEAD_SIZE)
        near_dk.append(
            jnp.einsum(
                "ail,aiz->alz",
                near_score_gradient,
                query_blocks,
                preferred_element_type=jnp.float32,
            )
            * softmax_scale
        )
        near_dv.append(
            jnp.einsum(
                "ail,aiz->alz", near_weight_rows, block_gradient, preferred_element_type=jnp.float32
            )
        )
        for level_idx in range(LEV):
            dp_far = jnp.einsum(
                "td,kd->tk", d_out, coarse_v[level_idx], preferred_element_type=jnp.float32
            )
            ds_far = (prob_far[level_idx] * (dp_far - delta[:, None])).astype(jnp.bfloat16)
            query_gradient = query_gradient + jnp.dot(
                ds_far, coarse_k[level_idx], preferred_element_type=jnp.float32
            )
            far_dk[level_idx].append(
                jnp.einsum("tk,td->kd", ds_far, q_head, preferred_element_type=jnp.float32)
                * softmax_scale
            )
            far_dv[level_idx].append(
                jnp.einsum(
                    "tk,td->kd", weight_far[level_idx], d_out, preferred_element_type=jnp.float32
                )
            )
        grad_q_list.append(query_gradient * softmax_scale)
    contrib = jnp.concatenate(near_dk + near_dv, axis=2).reshape(
        blocks_here * NEAR_SLOTS, BLOCK_TOKENS * columns
    )
    spread_ext = jnp.einsum(
        "xe,xc->ec", select_flat.astype(jnp.float32), contrib, precision=lax.Precision.HIGHEST
    )
    spread_ext = spread_ext.reshape(extended * BLOCK_TOKENS, columns)
    lower_rim = spread_ext[:margin]
    own_rows = spread_ext[margin : margin + tok_rows]
    upper_rim = spread_ext[margin + tok_rows :]
    from_above = passed_along(lower_rim.astype(jnp.bfloat16), "ctx", -1).astype(lower_rim.dtype)
    from_below = passed_along(upper_rim.astype(jnp.bfloat16), "ctx", 1).astype(upper_rim.dtype)
    grad_pair = own_rows + from_above + from_below
    far_grad = [
        jnp.concatenate(far_dk[level_idx] + far_dv[level_idx], axis=1) for level_idx in range(LEV)
    ]
    for bit_idx in reversed(range(steps_count)):
        active = [level_idx for level_idx in range(LEV) if groups[level_idx] > 2**bit_idx]
        upper_half = device // 2**bit_idx % 2 == 1
        sends = []
        keeps = []
        for level_idx in active:
            half_rows = far_grad[level_idx].shape[0] // 2
            lower_part = far_grad[level_idx][:half_rows]
            upper_part = far_grad[level_idx][half_rows:]
            keeps.append(jnp.where(upper_half, upper_part, lower_part))
            sends.append(jnp.where(upper_half, lower_part, upper_part))
        received = from_partner(shortened(jnp.concatenate(sends, axis=0)), "ctx", bit_idx)
        offset = 0
        for position, level_idx in enumerate(active):
            half_rows = keeps[position].shape[0]
            far_grad[level_idx] = keeps[position] + received[offset : offset + half_rows]
            offset = offset + half_rows
    for level_idx in range(LEV):
        factor = factors[level_idx]
        rows_level = far_grad[level_idx].shape[0]
        expanded = jnp.broadcast_to(
            (far_grad[level_idx] / factor)[:, None, :], (rows_level, factor, columns)
        )
        grad_pair = grad_pair + expanded.reshape(tok_rows, columns)
    grad_queries = jnp.concatenate(grad_q_list, axis=1).astype(jnp.bfloat16)
    grad_keys = grad_pair[:, :local_cols].astype(jnp.bfloat16)
    grad_values = grad_pair[:, local_cols:].astype(jnp.bfloat16)
    return (mixed, grad_queries, grad_keys, grad_values)


def solution(mesh):
    return jax.shard_map(
        body,
        mesh=mesh,
        in_specs=(
            P("ctx", "head"),
            P("ctx", "head"),
            P("ctx", "head"),
            P("ctx", None),
            P("ctx"),
            P("head"),
            P("head"),
            P("ctx", "head"),
        ),
        out_specs=(P("ctx", "head"), P("ctx", "head"), P("ctx", "head"), P("ctx", "head")),
        check_vma=False,
    )
```

profile of v0, /device:TPU:1, one launch (start us, length us, event | category | flops | bytes accessed | tf_op | source)
XLA Modules:
  0.0 259.7 jit_solution(10416025845603578630)
XLA Ops:
  7.2 1.0 concatenate.87
  8.3 1.0 concatenate.90
  9.3 1.0 concatenate.88
  10.3 1.0 concatenate.91
  13.6 4.5 %collective-permute-start = (bf16[256,512]{1,0:T(8,128)(2,1)S(1)}, bf16[256,512]{1,0:T(8,128)(2,1)S(1)}, u32[]{:S(2)}, u32[]{:S(2)}) collective-permute-start(bf16[256,512]{1,0:T(8,128)(2,1)S(1)} %constant_dynamic-update-slice_fusion), channel_id=1, source_target_pairs={{0,16},{16,32},{32,48},{48,64},{64,80},{80,96},{96,112},{112,128},... | collective-permute-start | bytes 786440 | tf_op jit(solution)/shard_map/ppermute | solution.py:26
  18.1 5.6 %collective-permute-start.1 = (bf16[256,512]{1,0:T(8,128)(2,1)S(1)}, bf16[256,512]{1,0:T(8,128)(2,1)S(1)}, u32[]{:S(2)}, u32[]{:S(2)}) collective-permute-start(bf16[256,512]{1,0:T(8,128)(2,1)S(1)} %constant_dynamic-update-slice_fusion), channel_id=1, source_target_pairs={{16,0},{32,16},{48,32},{64,48},{80,64},{96,80},{112,96},{128,112},... | collective-permute-start | bytes 786440 | tf_op jit(solution)/shard_map/ppermute | solution.py:28
  28.6 1.1 fusion.272
  30.2 56.8 %all-gather.2.cloned.1.call-done = bf16[7936,512]{1,0:T(8,128)(2,1)} async-done(((bf16[248,512]{1,0:T(8,128)(2,1)}), bf16[7936,512]{1,0:T(8,128)(2,1)}) %all-gather.2.cloned.1.call-update) | async-done | bytes 8126480 | tf_op jit(solution)/shard_map/all_gather | solution.py:109
  87.0 2.6 %slice.349 = bf16[32,128,512]{2,1,0:T(8,128)(2,1)S(1)} slice(bf16[32,248,512]{2,1,0:T(8,128)(2,1)} %bitcast.285), slice={[0:32], [0:128], [0:512]} | slice | bytes 8388608 | tf_op jit(solution)/shard_map/slice | solution.py:115
  89.7 1.8 slice.351
  91.5 1.3 slice.353
  92.8 1.1 slice.355
  93.9 1.0 slice_bitcast_fusion
  98.2 0.9 fusion.78
  101.5 1.1 fusion.101
  102.6 1.7 copy.148
  104.3 1.3 convolution_add_fusion.19
  105.6 1.3 convolution_add_fusion.18
  107.0 1.0 convolution_add_fusion.17
  108.0 1.0 convolution_add_fusion.16
  109.0 1.1 fusion.97
  110.1 1.7 copy.267
  111.8 1.2 convolution_add_fusion.14
  113.1 1.3 convolution_add_fusion.13
  114.4 1.0 convolution_add_fusion.12
  115.9 1.5 broadcast_multiply_fusion.1
  117.5 1.6 broadcast_multiply_fusion
  119.8 25.6 %all-reduce = (f32[256]{0:T(256)}, f32[256]{0:T(256)}) all-reduce(f32[256]{0:T(256)} %get-tuple-element.21, f32[256]{0:T(256)} %get-tuple-element.20), channel_id=1, replica_groups=mesh['ctx'=32,'head'=16] {'head'}, use_global_device_ids=true, to_apply=%region_30.31 | all-reduce | flops 512 | bytes 4096 | tf_op jit(solution)/shard_map/psum | solution.py:197
  146.2 1.8 subtract_multiply_fusion
  147.9 2.2 multiply_reduce_fusion.3
  150.2 1.9 fusion.130
  152.1 1.7 fusion.127
  153.8 0.9 fusion.115
  154.8 0.9 fusion.112
  165.5 1.0 fusion.289
  166.9 0.9 fusion.290
  172.3 4.4 %collective-permute-start.4 = (bf16[128,512]{1,0:T(8,128)(2,1)}, bf16[128,512]{1,0:T(8,128)(2,1)}, u32[]{:S(2)}, u32[]{:S(2)}) collective-permute-start(bf16[128,512]{1,0:T(8,128)(2,1)} %select_convert_fusion), channel_id=1, source_target_pairs={{0,256},{16,272},{32,288},{48,304},{64,320},{80,336},{96,352},{112... | collective-permute-start | bytes 393224 | tf_op jit(solution)/shard_map/ppermute | solution.py:52
  180.2 1.7 reshape.810
  181.9 2.8 %fusion.288 = (bf16[6,65536]{1,0:T(8,128)(2,1)S(1)}, f32[6,65536]{1,0:T(8,128)S(1)}) fusion(f32[8,65536]{1,0:T(8,128)} %reshape.810, s32[8]{0:T(128)S(1)} %copy-done.132), kind=kOutput, calls=%fused_computation.486 | convolution fusion | flops 38142000 | bytes 4456480 | tf_op jit(solution)/shard_map/xe,xc->ec/dot_general | solution.py:270
  185.0 0.9 convert_element_type.240
  186.0 9.1 %collective-permute-start.2 = (bf16[256,512]{1,0:T(8,128)(2,1)}, bf16[256,512]{1,0:T(8,128)(2,1)}, u32[]{:S(2)}, u32[]{:S(2)}) collective-permute-start(bf16[256,512]{1,0:T(8,128)(2,1)} %convert_element_type.240), channel_id=1, source_target_pairs={{16,0},{32,16},{48,32},{64,48},{80,64},{96,80},{112,96},{128,112},... | collective-permute-start | bytes 786440 | tf_op jit(solution)/shard_map/ppermute | solution.py:38
  196.0 2.1 collective-permute-start.3
  198.1 1.1 convolution_add_fusion.9
  199.3 1.2 convolution_add_fusion.8
  200.5 1.1 convolution_add_fusion.7
  201.6 1.1 convolution_add_fusion.6
  202.8 1.2 convolution_add_fusion.4
  204.0 1.1 convolution_add_fusion.3
  205.1 1.8 convolution_add_fusion.2
  207.3 1.1 convert_add_fusion.3
  208.5 2.2 collective-permute-start.5
  210.7 4.8 %collective-permute-done.5 = bf16[192,512]{1,0:T(8,128)(2,1)S(1)} collective-permute-done((bf16[192,512]{1,0:T(8,128)(2,1)S(1)}, bf16[192,512]{1,0:T(8,128)(2,1)S(1)}, u32[]{:S(2)}, u32[]{:S(2)}) %collective-permute-start.5) | collective-permute-done | bytes 196640 | tf_op jit(solution)/shard_map/ppermute | solution.py:52
  215.7 5.5 %collective-permute-start.6 = (bf16[224,512]{1,0:T(8,128)(2,1)S(1)}, bf16[224,512]{1,0:T(8,128)(2,1)S(1)}, u32[]{:S(2)}, u32[]{:S(2)}) collective-permute-start(bf16[224,512]{1,0:T(8,128)(2,1)S(1)} %pad_maximum_fusion.9), channel_id=1, source_target_pairs={{0,64},{16,80},{32,96},{48,112},{64,0},{80,16},{96,32},{112,48},{1... | collective-permute-start | bytes 688136 | tf_op jit(solution)/shard_map/ppermute | solution.py:52
  221.9 3.7 %collective-permute-done.6 = bf16[224,512]{1,0:T(8,128)(2,1)S(1)} collective-permute-done((bf16[224,512]{1,0:T(8,128)(2,1)S(1)}, bf16[224,512]{1,0:T(8,128)(2,1)S(1)}, u32[]{:S(2)}, u32[]{:S(2)}) %collective-permute-start.6) | collective-permute-done | bytes 229408 | tf_op jit(solution)/shard_map/ppermute | solution.py:52
  226.5 4.9 %collective-permute-start.7 = (bf16[240,512]{1,0:T(8,128)(2,1)}, bf16[240,512]{1,0:T(8,128)(2,1)}, u32[]{:S(2)}, u32[]{:S(2)}) collective-permute-start(bf16[240,512]{1,0:T(8,128)(2,1)} %pad_maximum_fusion.8), channel_id=1, source_target_pairs={{0,32},{16,48},{32,0},{48,16},{64,96},{80,112},{96,64},{112,80},{1... | collective-permute-start | bytes 737288 | tf_op jit(solution)/shard_map/ppermute | solution.py:52
  231.5 1.7 fusion.61
  233.2 1.1 slice.379
  234.3 1.5 slice.299
  235.8 1.7 copy.210
  237.5 1.2 convolution_add_fusion.1
  238.7 1.0 convert_add_fusion
  244.7 3.4 %collective-permute-start.8 = (bf16[248,512]{1,0:T(8,128)(2,1)}, bf16[248,512]{1,0:T(8,128)(2,1)S(1)}, u32[]{:S(2)}, u32[]{:S(2)}) collective-permute-start(bf16[248,512]{1,0:T(8,128)(2,1)} %constant_dynamic-update-slice_fusion.4), channel_id=1, source_target_pairs={{0,16},{16,0},{32,48},{48,32},{64,80},{80,64},{96,112},{112,96},{1... | collective-permute-start | bytes 761864 | tf_op jit(solution)/shard_map/ppermute | solution.py:52
  248.1 1.1 fusion.60
  250.9 1.3 fusion.62
  (443 shorter events, 42.7 us)
Async XLA Ops:
  7.2 79.8 %all-gather.2.cloned.1.call-start = ((), (), s32[]{:S(2)}) async-start(), calls=%async_computation | async-start | bytes 8380416 | tf_op jit(solution)/shard_map/all_gather | solution.py:109
  8.3 17.3 %copy-start.130 = (f32[2]{0:T(128)S(1)}, f32[2]{0:T(128)}, u32[]{:S(2)}) copy-start(f32[2]{0:T(128)} %param.13) | copy-start | bytes 28
  8.3 17.9 %copy-start.146 = (s32[2]{0:T(128)S(1)}, s32[2]{0:T(128)}, u32[]{:S(2)}) copy-start(s32[2]{0:T(128)} %param.12) | copy-start | bytes 28
  8.3 18.1 %copy-start.145 = (s32[2,4]{1,0:T(2,128)S(1)}, s32[2,4]{1,0:T(2,128)}, u32[]{:S(2)}) copy-start(s32[2,4]{1,0:T(2,128)} %param.11) | copy-start | bytes 100
  9.2 17.3 %copy-start.71 = (bf16[256,256]{1,0:T(8,128)(2,1)S(1)}, bf16[256,256]{1,0:T(8,128)(2,1)}, u32[]{:S(2)}) copy-start(bf16[256,256]{1,0:T(8,128)(2,1)} %param.15) | copy-start | bytes 393220
  10.3 16.5 %copy-start = (bf16[256,256]{1,0:T(8,128)(2,1)S(1)}, bf16[256,256]{1,0:T(8,128)(2,1)}, u32[]{:S(2)}) copy-start(bf16[256,256]{1,0:T(8,128)(2,1)} %param.8) | copy-start | bytes 393220
  13.6 13.2 %collective-permute-start = (bf16[256,512]{1,0:T(8,128)(2,1)S(1)}, bf16[256,512]{1,0:T(8,128)(2,1)S(1)}, u32[]{:S(2)}, u32[]{:S(2)}) collective-permute-start(bf16[256,512]{1,0:T(8,128)(2,1)S(1)} %constant_dynamic-update-slice_fusion), channel_id=1, source_target_pairs={{0,16},{16,32},{32,48},{48,64},{64,80},{80,96},{96,112},{112,128},... | collective-permute-start | bytes 786440 | tf_op jit(solution)/shard_map/ppermute | solution.py:26
  18.1 8.7 %collective-permute-start.1 = (bf16[256,512]{1,0:T(8,128)(2,1)S(1)}, bf16[256,512]{1,0:T(8,128)(2,1)S(1)}, u32[]{:S(2)}, u32[]{:S(2)}) collective-permute-start(bf16[256,512]{1,0:T(8,128)(2,1)S(1)} %constant_dynamic-update-slice_fusion), channel_id=1, source_target_pairs={{16,0},{32,16},{48,32},{64,48},{80,64},{96,80},{112,96},{128,112},... | collective-permute-start | bytes 786440 | tf_op jit(solution)/shard_map/ppermute | solution.py:28
  23.7 73.8 %copy-start.81 = (s32[256]{0:T(256)}, s32[256]{0:T(256)S(1)}, u32[]{:S(2)}) copy-start(s32[256]{0:T(256)S(1)} %and_select_fusion.12) | copy-start | bytes 3076
  23.8 72.0 %copy-start.86 = (s32[256]{0:T(256)}, s32[256]{0:T(256)S(1)}, u32[]{:S(2)}) copy-start(s32[256]{0:T(256)S(1)} %get-tuple-element.101) | copy-start | bytes 3076
  23.8 72.6 %copy-start.98 = (s32[256]{0:T(256)}, s32[256]{0:T(256)S(1)}, u32[]{:S(2)}) copy-start(s32[256]{0:T(256)S(1)} %get-tuple-element.100) | copy-start | bytes 3076
  23.8 72.5 %copy-start.101 = (s32[256]{0:T(256)}, s32[256]{0:T(256)S(1)}, u32[]{:S(2)}) copy-start(s32[256]{0:T(256)S(1)} %get-tuple-element.98) | copy-start | bytes 3076
  23.8 72.5 %copy-start.104 = (s32[256]{0:T(256)}, s32[256]{0:T(256)S(1)}, u32[]{:S(2)}) copy-start(s32[256]{0:T(256)S(1)} %get-tuple-element.99) | copy-start | bytes 3076
  25.0 70.7 %copy-start.111 = (s32[256]{0:T(256)}, s32[256]{0:T(256)S(1)}, u32[]{:S(2)}) copy-start(s32[256]{0:T(256)S(1)} %get-tuple-element.102) | copy-start | bytes 3076
  25.0 70.7 %copy-start.114 = (s32[256]{0:T(256)}, s32[256]{0:T(256)S(1)}, u32[]{:S(2)}) copy-start(s32[256]{0:T(256)S(1)} %get-tuple-element.103) | copy-start | bytes 3076
  26.4 68.8 %copy-start.133 = (s32[256]{0:T(256)}, s32[256]{0:T(256)S(1)}, u32[]{:S(2)}) copy-start(s32[256]{0:T(256)S(1)} %and_select_fusion.13) | copy-start | bytes 3076
  94.9 63.1 %copy-start.10 = (bf16[256,512]{1,0:T(8,128)(2,1)}, bf16[256,512]{1,0:T(8,128)(2,1)S(1)}, u32[]{:S(2)}) copy-start(bf16[256,512]{1,0:T(8,128)(2,1)S(1)} %slice_bitcast_fusion) | copy-start | bytes 786436
  94.9 68.7 %copy-start.7 = (bf16[2,128,512]{2,1,0:T(8,128)(2,1)}, bf16[2,128,512]{2,1,0:T(8,128)(2,1)S(1)}, u32[]{:S(2)}) copy-start(bf16[2,128,512]{2,1,0:T(8,128)(2,1)S(1)} %constant_dynamic-slice_fusion.3) | copy-start | bytes 786436
  95.2 16.6 %copy-start.40 = (f32[256,256]{0,1:T(8,128)}, f32[256,256]{0,1:T(8,128)S(1)}, u32[]{:S(2)}) copy-start(f32[256,256]{0,1:T(8,128)S(1)} %get-tuple-element.83) | copy-start | bytes 786436
  95.4 65.3 %copy-start.8 = (bf16[4,64,512]{2,1,0:T(8,128)(2,1)}, bf16[4,64,512]{2,1,0:T(8,128)(2,1)S(1)}, u32[]{:S(2)}) copy-start(bf16[4,64,512]{2,1,0:T(8,128)(2,1)S(1)} %constant_dynamic-slice_fusion.2) | copy-start | bytes 786436
  96.1 60.1 %copy-start.9 = (bf16[8,32,512]{2,1,0:T(8,128)(2,1)}, bf16[8,32,512]{2,1,0:T(8,128)(2,1)S(1)}, u32[]{:S(2)}) copy-start(bf16[8,32,512]{2,1,0:T(8,128)(2,1)S(1)} %constant_dynamic-slice_fusion.1) | copy-start | bytes 786436
  96.7 104.9 %copy-start.6 = (bf16[16,16,512]{2,1,0:T(8,128)(2,1)}, bf16[16,16,512]{2,1,0:T(8,128)(2,1)S(1)}, u32[]{:S(2)}) copy-start(bf16[16,16,512]{2,1,0:T(8,128)(2,1)S(1)} %constant_dynamic-slice_fusion) | copy-start | bytes 786436
  117.5 28.7 %copy-start.28 = (f32[256,128]{0,1:T(8,128)}, f32[256,128]{0,1:T(8,128)S(1)}, u32[]{:S(2)}) copy-start(f32[256,128]{0,1:T(8,128)S(1)} %get-tuple-element.88) | copy-start | bytes 393220
  119.1 27.1 %copy-start.29 = (f32[256,128]{0,1:T(8,128)}, f32[256,128]{0,1:T(8,128)S(1)}, u32[]{:S(2)}) copy-start(f32[256,128]{0,1:T(8,128)S(1)} %get-tuple-element.86) | copy-start | bytes 393220
  146.1 7.7 %copy-start.50 = (f32[256,256]{0,1:T(8,128)S(1)}, f32[256,256]{0,1:T(8,128)}, u32[]{:S(2)}) copy-start(f32[256,256]{0,1:T(8,128)} %copy-done.48) | copy-start | bytes 786436
  146.1 7.7 %copy-start.85 = (s32[256]{0:T(256)S(1)}, s32[256]{0:T(256)}, u32[]{:S(2)}) copy-start(s32[256]{0:T(256)} %copy-done.81) | copy-start | bytes 3076
  146.1 7.7 %copy-start.100 = (s32[256]{0:T(256)S(1)}, s32[256]{0:T(256)}, u32[]{:S(2)}) copy-start(s32[256]{0:T(256)} %copy-done.98) | copy-start | bytes 3076
  146.2 7.7 %copy-start.103 = (s32[256]{0:T(256)S(1)}, s32[256]{0:T(256)}, u32[]{:S(2)}) copy-start(s32[256]{0:T(256)} %copy-done.101) | copy-start | bytes 3076
  155.9 11.9 %copy-start.22 = (bf16[256,256]{0,1:T(8,128)(2,1)}, bf16[256,256]{0,1:T(8,128)(2,1)S(1)}, u32[]{:S(2)}) copy-start(bf16[256,256]{0,1:T(8,128)(2,1)S(1)} %fusion.50) | copy-start | bytes 393220
  156.2 13.3 %copy-start.21 = (bf16[256,256]{0,1:T(8,128)(2,1)}, bf16[256,256]{0,1:T(8,128)(2,1)S(1)}, u32[]{:S(2)}) copy-start(bf16[256,256]{0,1:T(8,128)(2,1)S(1)} %fusion.51) | copy-start | bytes 393220
  156.4 12.2 %copy-start.19 = (bf16[256,256]{0,1:T(8,128)(2,1)}, bf16[256,256]{0,1:T(8,128)(2,1)S(1)}, u32[]{:S(2)}) copy-start(bf16[256,256]{0,1:T(8,128)(2,1)S(1)} %fusion.55) | copy-start | bytes 393220
  157.2 13.2 %copy-start.16 = (bf16[256,256]{0,1:T(8,128)(2,1)}, bf16[256,256]{0,1:T(8,128)(2,1)S(1)}, u32[]{:S(2)}) copy-start(bf16[256,256]{0,1:T(8,128)(2,1)S(1)} %fusion.56) | copy-start | bytes 393220
  158.0 13.2 %copy-start.17 = (bf16[256,256]{0,1:T(8,128)(2,1)}, bf16[256,256]{0,1:T(8,128)(2,1)S(1)}, u32[]{:S(2)}) copy-start(bf16[256,256]{0,1:T(8,128)(2,1)S(1)} %fusion.52) | copy-start | bytes 393220
  158.7 12.6 %copy-start.14 = (bf16[256,256]{0,1:T(8,128)(2,1)}, bf16[256,256]{0,1:T(8,128)(2,1)S(1)}, u32[]{:S(2)}) copy-start(bf16[256,256]{0,1:T(8,128)(2,1)S(1)} %fusion.57) | copy-start | bytes 393220
  160.8 15.9 %copy-start.25 = (bf16[256,256]{0,1:T(8,128)(2,1)}, bf16[256,256]{0,1:T(8,128)(2,1)S(1)}, u32[]{:S(2)}) copy-start(bf16[256,256]{0,1:T(8,128)(2,1)S(1)} %fusion.49) | copy-start | bytes 393220
  161.5 16.0 %copy-start.23 = (bf16[256,256]{0,1:T(8,128)(2,1)}, bf16[256,256]{0,1:T(8,128)(2,1)S(1)}, u32[]{:S(2)}) copy-start(bf16[256,256]{0,1:T(8,128)(2,1)S(1)} %fusion.54) | copy-start | bytes 393220
  163.6 14.8 %copy-start.27 = (bf16[256,256]{0,1:T(8,128)(2,1)}, bf16[256,256]{0,1:T(8,128)(2,1)S(1)}, u32[]{:S(2)}) copy-start(bf16[256,256]{0,1:T(8,128)(2,1)S(1)} %fusion.48) | copy-start | bytes 393220
  163.8 15.4 %copy-start.26 = (bf16[256,256]{0,1:T(8,128)(2,1)}, bf16[256,256]{0,1:T(8,128)(2,1)S(1)}, u32[]{:S(2)}) copy-start(bf16[256,256]{0,1:T(8,128)(2,1)S(1)} %fusion.53) | copy-start | bytes 393220
  172.3 35.1 %collective-permute-start.4 = (bf16[128,512]{1,0:T(8,128)(2,1)}, bf16[128,512]{1,0:T(8,128)(2,1)}, u32[]{:S(2)}, u32[]{:S(2)}) collective-permute-start(bf16[128,512]{1,0:T(8,128)(2,1)} %select_convert_fusion), channel_id=1, source_target_pairs={{0,256},{16,272},{32,288},{48,304},{64,320},{80,336},{96,352},{112... | collective-permute-start | bytes 393224 | tf_op jit(solution)/shard_map/ppermute | solution.py:52
  184.6 13.4 %copy-start.12 = (f32[2,128,128]{2,1,0:T(8,128)S(1)}, f32[2,128,128]{2,1,0:T(8,128)}, u32[]{:S(2)}) copy-start(f32[2,128,128]{2,1,0:T(8,128)} %fusion.289) | copy-start | bytes 393220
  186.0 16.8 %copy-start.13 = (f32[2,128,128]{2,1,0:T(8,128)S(1)}, f32[2,128,128]{2,1,0:T(8,128)}, u32[]{:S(2)}) copy-start(f32[2,128,128]{2,1,0:T(8,128)} %fusion.290) | copy-start | bytes 393220
  186.0 64.9 %collective-permute-start.2 = (bf16[256,512]{1,0:T(8,128)(2,1)}, bf16[256,512]{1,0:T(8,128)(2,1)}, u32[]{:S(2)}, u32[]{:S(2)}) collective-permute-start(bf16[256,512]{1,0:T(8,128)(2,1)} %convert_element_type.240), channel_id=1, source_target_pairs={{16,0},{32,16},{48,32},{64,48},{80,64},{96,80},{112,96},{128,112},... | collective-permute-start | bytes 786440 | tf_op jit(solution)/shard_map/ppermute | solution.py:38
  196.0 8.0 %copy-start.24 = (bf16[256,256]{0,1:T(8,128)(2,1)S(1)}, bf16[256,256]{0,1:T(8,128)(2,1)}, u32[]{:S(2)}) copy-start(bf16[256,256]{0,1:T(8,128)(2,1)} %copy-done.23) | copy-start | bytes 393220
  196.0 9.1 %copy-start.20 = (bf16[256,256]{0,1:T(8,128)(2,1)S(1)}, bf16[256,256]{0,1:T(8,128)(2,1)}, u32[]{:S(2)}) copy-start(bf16[256,256]{0,1:T(8,128)(2,1)} %copy-done.19) | copy-start | bytes 393220
  196.0 10.9 %copy-start.32 = (f32[256,128]{1,0:T(8,128)S(1)}, f32[256,128]{1,0:T(8,128)}, u32[]{:S(2)}) copy-start(f32[256,128]{1,0:T(8,128)} %convolution_multiply_fusion.19) | copy-start | bytes 393220
  196.0 10.9 %copy-start.33 = (f32[256,128]{1,0:T(8,128)S(1)}, f32[256,128]{1,0:T(8,128)}, u32[]{:S(2)}) copy-start(f32[256,128]{1,0:T(8,128)} %convolution_multiply_fusion.18) | copy-start | bytes 393220
  196.0 10.9 %copy-start.74 = (f32[256,128]{1,0:T(8,128)S(1)}, f32[256,128]{1,0:T(8,128)}, u32[]{:S(2)}) copy-start(f32[256,128]{1,0:T(8,128)} %fusion.130) | copy-start | bytes 393220
  196.0 10.9 %copy-start.75 = (f32[256,128]{1,0:T(8,128)S(1)}, f32[256,128]{1,0:T(8,128)}, u32[]{:S(2)}) copy-start(f32[256,128]{1,0:T(8,128)} %fusion.115) | copy-start | bytes 393220
  196.0 54.8 %collective-permute-start.3 = (bf16[256,512]{1,0:T(8,128)(2,1)}, bf16[256,512]{1,0:T(8,128)(2,1)}, u32[]{:S(2)}, u32[]{:S(2)}) collective-permute-start(bf16[256,512]{1,0:T(8,128)(2,1)} %convert_element_type.242), channel_id=1, source_target_pairs={{0,16},{16,32},{32,48},{48,64},{64,80},{80,96},{96,112},{112,128},... | collective-permute-start | bytes 786440 | tf_op jit(solution)/shard_map/ppermute | solution.py:38
  199.2 7.8 %copy-start.30 = (f32[256,128]{1,0:T(8,128)S(1)}, f32[256,128]{1,0:T(8,128)}, u32[]{:S(2)}) copy-start(f32[256,128]{1,0:T(8,128)} %convolution_multiply_fusion.17) | copy-start | bytes 393220
  199.2 7.8 %copy-start.31 = (f32[256,128]{1,0:T(8,128)S(1)}, f32[256,128]{1,0:T(8,128)}, u32[]{:S(2)}) copy-start(f32[256,128]{1,0:T(8,128)} %convolution_multiply_fusion.16) | copy-start | bytes 393220
  199.2 7.8 %copy-start.72 = (f32[256,128]{1,0:T(8,128)S(1)}, f32[256,128]{1,0:T(8,128)}, u32[]{:S(2)}) copy-start(f32[256,128]{1,0:T(8,128)} %fusion.127) | copy-start | bytes 393220
  199.3 7.8 %copy-start.73 = (f32[256,128]{1,0:T(8,128)S(1)}, f32[256,128]{1,0:T(8,128)}, u32[]{:S(2)}) copy-start(f32[256,128]{1,0:T(8,128)} %fusion.112) | copy-start | bytes 393220
  207.3 8.4 %copy-start.3 = (f32[256,512]{1,0:T(8,128)}, f32[256,512]{1,0:T(8,128)S(1)}, u32[]{:S(2)}) copy-start(f32[256,512]{1,0:T(8,128)S(1)} %pad_maximum_fusion.3) | copy-start | bytes 1572868
  208.5 7.1 %collective-permute-start.5 = (bf16[192,512]{1,0:T(8,128)(2,1)S(1)}, bf16[192,512]{1,0:T(8,128)(2,1)S(1)}, u32[]{:S(2)}, u32[]{:S(2)}) collective-permute-start(bf16[192,512]{1,0:T(8,128)(2,1)S(1)} %pad_maximum_fusion.10), channel_id=1, source_target_pairs={{0,128},{16,144},{32,160},{48,176},{64,192},{80,208},{96,224},{112... | collective-permute-start | bytes 589832 | tf_op jit(solution)/shard_map/ppermute | solution.py:52
  215.6 15.9 %copy-start.18 = (bf16[256,256]{0,1:T(8,128)(2,1)S(1)}, bf16[256,256]{0,1:T(8,128)(2,1)}, u32[]{:S(2)}) copy-start(bf16[256,256]{0,1:T(8,128)(2,1)} %copy-done.17) | copy-start | bytes 393220
  215.7 9.9 %collective-permute-start.6 = (bf16[224,512]{1,0:T(8,128)(2,1)S(1)}, bf16[224,512]{1,0:T(8,128)(2,1)S(1)}, u32[]{:S(2)}, u32[]{:S(2)}) collective-permute-start(bf16[224,512]{1,0:T(8,128)(2,1)S(1)} %pad_maximum_fusion.9), channel_id=1, source_target_pairs={{0,64},{16,80},{32,96},{48,112},{64,0},{80,16},{96,32},{112,48},{1... | collective-permute-start | bytes 688136 | tf_op jit(solution)/shard_map/ppermute | solution.py:52
  225.7 14.0 %copy-start.5 = (f32[64,512]{1,0:T(8,128)}, f32[64,512]{1,0:T(8,128)S(1)}, u32[]{:S(2)}) copy-start(f32[64,512]{1,0:T(8,128)S(1)} %convert_add_fusion.5) | copy-start | bytes 393220
  225.7 13.0 %copy-start.4 = (f32[256,512]{1,0:T(8,128)S(1)}, f32[256,512]{1,0:T(8,128)}, u32[]{:S(2)}) copy-start(f32[256,512]{1,0:T(8,128)} %copy-done.3) | copy-start | bytes 1572868
  226.5 12.2 %collective-permute-start.7 = (bf16[240,512]{1,0:T(8,128)(2,1)}, bf16[240,512]{1,0:T(8,128)(2,1)}, u32[]{:S(2)}, u32[]{:S(2)}) collective-permute-start(bf16[240,512]{1,0:T(8,128)(2,1)} %pad_maximum_fusion.8), channel_id=1, source_target_pairs={{0,32},{16,48},{32,0},{48,16},{64,96},{80,112},{96,64},{112,80},{1... | collective-permute-start | bytes 737288 | tf_op jit(solution)/shard_map/ppermute | solution.py:52
  234.3 9.1 %copy-start.39 = (f32[32,512]{1,0:T(8,128)S(1)}, f32[32,512]{1,0:T(8,128)}, u32[]{:S(2)}) copy-start(f32[32,512]{1,0:T(8,128)} %copy-done.38) | copy-start | bytes 196612
  234.3 13.8 %copy-start.15 = (bf16[256,256]{0,1:T(8,128)(2,1)S(1)}, bf16[256,256]{0,1:T(8,128)(2,1)}, u32[]{:S(2)}) copy-start(bf16[256,256]{0,1:T(8,128)(2,1)} %copy-done.14) | copy-start | bytes 393220
  234.3 14.9 %copy-start.66 = (bf16[256,128]{1,0:T(8,128)(2,1)S(1)}, bf16[256,128]{1,0:T(8,128)(2,1)}, u32[]{:S(2)}) copy-start(bf16[256,128]{1,0:T(8,128)(2,1)} %fusion.61) | copy-start | bytes 196612
  244.7 5.2 %collective-permute-start.8 = (bf16[248,512]{1,0:T(8,128)(2,1)}, bf16[248,512]{1,0:T(8,128)(2,1)S(1)}, u32[]{:S(2)}, u32[]{:S(2)}) collective-permute-start(bf16[248,512]{1,0:T(8,128)(2,1)} %constant_dynamic-update-slice_fusion.4), channel_id=1, source_target_pairs={{0,16},{16,0},{32,48},{48,32},{64,80},{80,64},{96,112},{112,96},{1... | collective-permute-start | bytes 761864 | tf_op jit(solution)/shard_map/ppermute | solution.py:52
  (94 other events, 267.5 us)
Sparse Core Ops, SparseCore 0:
  13.6 73.3 all-gather.1
where the time goes:
time: 261 us; the launch traced here: 260 us
  waiting for transfers between devices  65.4 us (25%)
  matrix products  55.1 us (21%)
  starting transfers between devices  41.8 us (16%)
  local copies, waits for them, and re-layouts  30.9 us (12%)
  blocking collectives  25.6 us (10%)
  other arithmetic  24.1 us (9%)
  between operations  16.8 us (6%)
    all_gather x1, waiting for transfers between devices, body(): lax.all_gather(packed, 'ctx', axis=0, tiled=True)  56.8 us
    psum x1, blocking collectives, body(): squares = lax.psum(jnp.sum(scaled * scaled, axis=1), 'head')  25.6 us
    ppermute x5, starting transfers between devices, from_partner(): return lax.ppermute(value, axis, pairs)  20.5 us
    dot_general x10, matrix products, body(): jnp.dot(ds_far, coarse_k[level_idx], preferred_element_type=jnp.float32)  12.6 us
    dot_general x10, matrix products, body(): jnp.dot(weights_bf, coarse_v[level_idx], preferred_element_type=jnp.float32)  11.6 us
    ppermute x2, starting transfers between devices, passed_along(): return lax.ppermute(value, axis, pairs)  11.2 us
    dot_general x10, matrix products, body(): jnp.einsum('tk,td->kd', weight_far[level_idx], d_out, preferred_element_t...  9.72 us
    ppermute x5, waiting for transfers between devices, from_partner(): return lax.ppermute(value, axis, pairs)  8.53 us
  transfers between devices with their start and end apart: 10, of which 3 were waited for; matrix products, arithmetic and copies ran while one was open for 17% of the time, Pallas kernels for 0%

commit v1 on v0

--- a/solution.py
+++ b/solution.py
@@ -13,6 +13,18 @@
 LOG_TWO = 0.6931471805599453
 NEG_BIG = -1e30
 NORM_EPS = 1e-05
+
+
+def doubled_up(shard, axis, dim):
+    ways, here, hop = (lax.axis_size(axis), lax.axis_index(axis), shard.shape[dim])
+    line, have = (shard, 1)
+    while have < ways:
+        line = jnp.concatenate(
+            [line, lax.ppermute(line, axis, [(d, (d - have) % ways) for d in range(ways)])],
+            axis=dim,
+        )
+        have = 2 * have
+    return jnp.roll(line, here * hop, axis=dim)
 
 
 def padded_2(cells, sides, width):
@@ -106,9 +118,7 @@
     group_pair = list(pooled)
     shared = [level_idx for level_idx in range(LEV) if groups[level_idx] > 1]
     packed = jnp.concatenate([pooled[level_idx] for level_idx in shared], axis=0)
-    everyone = lax.all_gather(packed, "ctx", axis=0, tiled=True).reshape(
-        ctx_count, packed.shape[0], columns
-    )
+    everyone = doubled_up(packed, "ctx", 0).reshape(ctx_count, packed.shape[0], columns)
     offset = 0
     for level_idx in shared:
         count_rows = pooled[level_idx].shape[0]

time: 261 us -> 399 us (1.53)
  waiting for transfers between devices: 65.4 us -> 156 us
  starting transfers between devices: 41.8 us -> 63.2 us
  local copies, waits for them, and re-layouts: 30.9 us -> 50.3 us
  between operations: 16.8 us -> 3.16 us
  other arithmetic: 24.1 us -> 31.7 us
  matrix products: 55.1 us -> 62 us
  blocking collectives: 25.6 us -> 30 us
    ppermute x0 -> x5, waiting for transfers between devices: none -> 147 us  [doubled_up(): lax.ppermute(line, axis, [(d, (d - have) % ways) for d in range(ways)])]
    all_gather x1 -> x0, waiting for transfers between devices: 56.8 us -> none  [body(): lax.all_gather(packed, 'ctx', axis=0, tiled=True)]
    ppermute x0 -> x5, starting transfers between devices: none -> 25.9 us  [doubled_up(): lax.ppermute(line, axis, [(d, (d - have) % ways) for d in range(ways)])]
    unnamed x302 -> x294, local copies, waits for them, and re-layouts: 4.99 us -> 22.6 us
    concatenate x0 -> x2, local copies, waits for them, and re-layouts: none -> 6.68 us  [the longest x1 4.3 us: doubled_up(): return jnp.roll(line, here * hop, axis=dim)]
    slice x4, local copies, waits for them, and re-layouts: 6.85 us -> 0.99 us  [body(): piece = everyone[:, offset:offset + count_rows]]
    dynamic_slice x0 -> x1, local copies, waits for them, and re-layouts: none -> 5.37 us  [doubled_up(): return jnp.roll(line, here * hop, axis=dim)]
    psum x1, blocking collectives: 25.6 us -> 30 us  [body(): squares = lax.psum(jnp.sum(scaled * scaled, axis=1), 'head')]
  transfers between devices with their start and end apart: 10 -> 14, of which waited for: 3 -> 7; matrix products, arithmetic and copies ran while one was open for 17% -> 13% of each run, Pallas kernels for 0% -> 0%
where the time goes in v1:
time: 399 us; the launch traced here: 397 us
  waiting for transfers between devices  156 us (39%)
  starting transfers between devices  63.2 us (16%)
  matrix products  62 us (16%)
  local copies, waits for them, and re-layouts  50.3 us (13%)
  other arithmetic  31.7 us (8%)
  blocking collectives  30 us (8%)
    ppermute x5, waiting for transfers between devices, doubled_up(): lax.ppermute(line, axis, [(d, (d - have) % ways) for d in range(ways)])  147 us
    psum x1, blocking collectives, body(): squares = lax.psum(jnp.sum(scaled * scaled, axis=1), 'head')  30 us
    ppermute x5, starting transfers between devices, doubled_up(): lax.ppermute(line, axis, [(d, (d - have) % ways) for d in range(ways)])  25.9 us
    unnamed x294, local copies, waits for them, and re-layouts  22.6 us
    ppermute x5, starting transfers between devices, from_partner(): return lax.ppermute(value, axis, pairs)  17.6 us
    ppermute x2, starting transfers between devices, passed_along(): return lax.ppermute(value, axis, pairs)  13.1 us
    dot_general x10, matrix products, body(): jnp.dot(ds_far, coarse_k[level_idx], preferred_element_type=jnp.float32)  12.7 us
    dot_general x10, matrix products, body(): jnp.dot(weights_bf, coarse_v[level_idx], preferred_element_type=jnp.float32)  12.7 us
  transfers between devices with their start and end apart: 14, of which 7 were waited for; matrix products, arithmetic and copies ran while one was open for 13% of the time, Pallas kernels for 0%

profile of v1, /device:TPU:1, one launch (start us, length us, event | category | flops | bytes accessed | tf_op | source)
XLA Modules:
  0.0 396.6 jit_solution(2154534933925610533)
XLA Ops:
  7.6 1.1 convert_reduce_fusion.2
  13.2 8.8 %collective-permute-start.2 = (bf16[248,512]{1,0:T(8,128)(2,1)S(1)}, bf16[248,512]{1,0:T(8,128)(2,1)S(1)}, u32[]{:S(2)}, u32[]{:S(2)}) collective-permute-start(bf16[248,512]{1,0:T(8,128)(2,1)S(1)} %get-tuple-element.106), channel_id=1, source_target_pairs={{0,496},{16,0},{32,16},{48,32},{64,48},{80,64},{96,80},{112,96},{1... | collective-permute-start | bytes 761864 | tf_op jit(solution)/shard_map/ppermute | solution.py:23
  22.0 1.1 collective-permute-done.2
  24.0 9.4 %collective-permute-start.3 = (bf16[496,512]{1,0:T(8,128)(2,1)S(1)}, bf16[496,512]{1,0:T(8,128)(2,1)S(1)}, u32[]{:S(2)}, u32[]{:S(2)}) collective-permute-start(bf16[496,512]{1,0:T(8,128)(2,1)S(1)} %get-tuple-element.79), channel_id=1, source_target_pairs={{0,480},{16,496},{32,0},{48,16},{64,32},{80,48},{96,64},{112,80},{... | collective-permute-start | bytes 1523720 | tf_op jit(solution)/shard_map/ppermute | solution.py:23
  33.4 6.8 %collective-permute-done.3 = bf16[496,512]{1,0:T(8,128)(2,1)S(1)} collective-permute-done((bf16[496,512]{1,0:T(8,128)(2,1)S(1)}, bf16[496,512]{1,0:T(8,128)(2,1)S(1)}, u32[]{:S(2)}, u32[]{:S(2)}) %collective-permute-start.3) | collective-permute-done | bytes 507936 | tf_op jit(solution)/shard_map/ppermute | solution.py:23
  40.2 1.2 constant_dynamic-update-slice_fusion.30
  41.4 3.8 collective-permute-start.4
  45.2 23.9 %collective-permute-done.4 = bf16[992,512]{1,0:T(8,128)(2,1)S(1)} collective-permute-done((bf16[992,512]{1,0:T(8,128)(2,1)S(1)}, bf16[992,512]{1,0:T(8,128)(2,1)S(1)}, u32[]{:S(2)}, u32[]{:S(2)}) %collective-permute-start.4) | collective-permute-done | bytes 1015840 | tf_op jit(solution)/shard_map/ppermute | solution.py:23
  69.1 1.6 constant_dynamic-update-slice_fusion.29
  70.8 2.1 collective-permute-start.5
  72.9 45.2 %collective-permute-done.5 = bf16[1984,512]{1,0:T(8,128)(2,1)S(1)} collective-permute-done((bf16[1984,512]{1,0:T(8,128)(2,1)S(1)}, bf16[1984,512]{1,0:T(8,128)(2,1)S(1)}, u32[]{:S(2)}, u32[]{:S(2)}) %collective-permute-start.5) | collective-permute-done | bytes 2031648 | tf_op jit(solution)/shard_map/ppermute | solution.py:23
  118.1 2.4 constant_dynamic-update-slice_fusion.28
  120.5 1.9 collective-permute-start.6
  122.4 4.5 %collective-permute-start = (bf16[256,512]{1,0:T(8,128)(2,1)S(1)}, bf16[256,512]{1,0:T(8,128)(2,1)S(1)}, u32[]{:S(2)}, u32[]{:S(2)}) collective-permute-start(bf16[256,512]{1,0:T(8,128)(2,1)S(1)} %constant_dynamic-update-slice_fusion), channel_id=1, source_target_pairs={{0,16},{16,32},{32,48},{48,64},{64,80},{80,96},{96,112},{112,128},... | collective-permute-start | bytes 786440 | tf_op jit(solution)/shard_map/ppermute | solution.py:38
  126.9 2.1 collective-permute-start.1
  136.9 2.0 reshape.786
  139.0 1.1 convolution_convert_fusion
  140.4 1.1 fusion.267
  141.5 1.6 fusion.282
  143.1 1.6 fusion.276
  144.7 70.2 %collective-permute-done.6 = bf16[3968,512]{1,0:T(8,128)(2,1)} collective-permute-done((bf16[3968,512]{1,0:T(8,128)(2,1)}, bf16[3968,512]{1,0:T(8,128)(2,1)}, u32[]{:S(2)}, u32[]{:S(2)}) %collective-permute-start.6) | collective-permute-done | bytes 4063264 | tf_op jit(solution)/shard_map/ppermute | solution.py:23
  214.9 4.5 %constant_dynamic-update-slice_fusion.47 = bf16[15872,512]{1,0:T(8,128)(2,1)} fusion(bf16[15872,512]{1,0:T(8,128)(2,1)} %get-tuple-element.55, bf16[3968,512]{1,0:T(8,128)(2,1)} %collective-permute-done.6), kind=kLoop, calls=%fused_computation.273 | loop fusion | bytes 8126464
  225.2 1.5 constant_dynamic-update-slice_fusion.38
  226.7 4.3 %constant_dynamic-update-slice_fusion.37 = bf16[15872,512]{1,0:T(8,128)(2,1)} fusion(bf16[15872,512]{1,0:T(8,128)(2,1)} %constant_dynamic-update-slice_fusion.38, bf16[3968,512]{1,0:T(8,128)(2,1)} %collective-permute-done.6), kind=kLoop, calls=%fused_computation.263 | loop fusion | bytes 8126464 | tf_op jit(solution)/shard_map/jit(_roll_dynamic)/concatenate | solution.py:27
  231.0 5.4 %constant_dynamic-slice_fusion.4 = bf16[7936,512]{1,0:T(8,128)(2,1)S(1)} fusion(bf16[15872,512]{1,0:T(8,128)(2,1)} %constant_dynamic-update-slice_fusion.37, s32[]{:T(128)S(6)} %select_n.440), kind=kLoop, calls=%fused_computation.440 | loop fusion | bytes 16252932 | tf_op jit(solution)/shard_map/jit(_roll_dynamic)/dynamic_slice | solution.py:27
  246.3 1.3 convolution_add_fusion.17
  247.6 1.7 convolution_add_fusion.16
  249.3 1.4 fusion.96
  254.0 1.3 convolution_add_fusion.11
  255.3 1.9 broadcast_multiply_fusion.1
  257.3 1.5 broadcast_multiply_fusion
  259.5 30.0 %all-reduce = (f32[256]{0:T(256)}, f32[256]{0:T(256)}) all-reduce(f32[256]{0:T(256)} %get-tuple-element.21, f32[256]{0:T(256)} %get-tuple-element.20), channel_id=1, replica_groups=mesh['ctx'=32,'head'=16] {'head'}, use_global_device_ids=true, to_apply=%region_30.31 | all-reduce | flops 512 | bytes 4096 | tf_op jit(solution)/shard_map/psum | solution.py:207
  290.3 1.5 subtract_multiply_fusion
  291.7 2.2 multiply_reduce_fusion.3
  293.9 1.9 fusion.127
  295.9 1.9 fusion.124
  297.8 1.6 fusion.112
  299.4 1.7 fusion.109
  317.1 1.9 collective-permute-start.9
  322.5 1.7 reshape.810
  324.2 2.8 fusion.283
  328.3 11.0 %collective-permute-start.7 = (bf16[256,512]{1,0:T(8,128)(2,1)}, bf16[256,512]{1,0:T(8,128)(2,1)}, u32[]{:S(2)}, u32[]{:S(2)}) collective-permute-start(bf16[256,512]{1,0:T(8,128)(2,1)} %convert_element_type.240), channel_id=1, source_target_pairs={{16,0},{32,16},{48,32},{64,48},{80,64},{96,80},{112,96},{128,112},... | collective-permute-start | bytes 786440 | tf_op jit(solution)/shard_map/ppermute | solution.py:50
  340.3 2.1 collective-permute-start.8
  342.4 1.1 convolution_add_fusion.9
  343.5 1.1 convolution_add_fusion.8
  344.7 1.1 convolution_add_fusion.7
  345.8 1.1 convolution_add_fusion.6
  347.0 1.2 convolution_add_fusion.4
  348.2 1.1 convolution_add_fusion.3
  349.3 1.8 convolution_add_fusion.2
  351.1 1.1 pad_maximum_fusion.4
  352.6 1.1 convert_add_fusion.3
  353.8 2.3 collective-permute-start.10
  356.2 4.7 %collective-permute-done.10 = bf16[192,512]{1,0:T(8,128)(2,1)S(1)} collective-permute-done((bf16[192,512]{1,0:T(8,128)(2,1)S(1)}, bf16[192,512]{1,0:T(8,128)(2,1)S(1)}, u32[]{:S(2)}, u32[]{:S(2)}) %collective-permute-start.10) | collective-permute-done | bytes 196640 | tf_op jit(solution)/shard_map/ppermute | solution.py:64
  361.1 6.2 %collective-permute-start.11 = (bf16[224,512]{1,0:T(8,128)(2,1)S(1)}, bf16[224,512]{1,0:T(8,128)(2,1)S(1)}, u32[]{:S(2)}, u32[]{:S(2)}) collective-permute-start(bf16[224,512]{1,0:T(8,128)(2,1)S(1)} %pad_maximum_fusion.9), channel_id=1, source_target_pairs={{0,64},{16,80},{32,96},{48,112},{64,0},{80,16},{96,32},{112,48},{1... | collective-permute-start | bytes 688136 | tf_op jit(solution)/shard_map/ppermute | solution.py:64
  368.0 4.2 %collective-permute-done.11 = bf16[224,512]{1,0:T(8,128)(2,1)S(1)} collective-permute-done((bf16[224,512]{1,0:T(8,128)(2,1)S(1)}, bf16[224,512]{1,0:T(8,128)(2,1)S(1)}, u32[]{:S(2)}, u32[]{:S(2)}) %collective-permute-start.11) | collective-permute-done | bytes 229408 | tf_op jit(solution)/shard_map/ppermute | solution.py:64
  373.1 3.2 collective-permute-start.12
  376.3 1.7 fusion.61
  378.7 1.7 copy.238
  380.4 1.2 convolution_add_fusion.1
  381.7 1.1 convert_add_fusion
  387.8 3.9 collective-permute-start.13
  391.7 1.1 fusion.60
  394.6 1.3 fusion.62
  (444 shorter events, 71.2 us)
Async XLA Ops:
  0.6 8.7 %copy-start.1 = (bf16[256,256]{1,0:T(8,128)(2,1)S(1)}, bf16[256,256]{1,0:T(8,128)(2,1)}, u32[]{:S(2)}) copy-start(bf16[256,256]{1,0:T(8,128)(2,1)} %param.9) | copy-start | bytes 393220
  0.6 8.7 %copy-start.2 = (bf16[256,256]{1,0:T(8,128)(2,1)S(1)}, bf16[256,256]{1,0:T(8,128)(2,1)}, u32[]{:S(2)}) copy-start(bf16[256,256]{1,0:T(8,128)(2,1)} %param.10) | copy-start | bytes 393220
  9.4 59.8 %copy-start.47 = (bf16[32,512]{1,0:T(8,128)(2,1)}, bf16[32,512]{1,0:T(8,128)(2,1)S(1)}, u32[]{:S(2)}) copy-start(bf16[32,512]{1,0:T(8,128)(2,1)S(1)} %get-tuple-element.49) | copy-start | bytes 98308
  10.7 58.4 %copy-start.81 = (bf16[8,512]{1,0:T(8,128)(2,1)}, bf16[8,512]{1,0:T(8,128)(2,1)S(1)}, u32[]{:S(2)}) copy-start(bf16[8,512]{1,0:T(8,128)(2,1)S(1)} %get-tuple-element.45) | copy-start | bytes 24580
  13.2 9.9 %collective-permute-start.2 = (bf16[248,512]{1,0:T(8,128)(2,1)S(1)}, bf16[248,512]{1,0:T(8,128)(2,1)S(1)}, u32[]{:S(2)}, u32[]{:S(2)}) collective-permute-start(bf16[248,512]{1,0:T(8,128)(2,1)S(1)} %get-tuple-element.106), channel_id=1, source_target_pairs={{0,496},{16,0},{32,16},{48,32},{64,48},{80,64},{96,80},{112,96},{1... | collective-permute-start | bytes 761864 | tf_op jit(solution)/shard_map/ppermute | solution.py:23
  23.1 47.6 %copy-start.15 = (bf16[248,512]{1,0:T(8,128)(2,1)}, bf16[248,512]{1,0:T(8,128)(2,1)S(1)}, u32[]{:S(2)}) copy-start(bf16[248,512]{1,0:T(8,128)(2,1)S(1)} %collective-permute-done.2) | copy-start | bytes 761860
  24.0 16.2 %collective-permute-start.3 = (bf16[496,512]{1,0:T(8,128)(2,1)S(1)}, bf16[496,512]{1,0:T(8,128)(2,1)S(1)}, u32[]{:S(2)}, u32[]{:S(2)}) collective-permute-start(bf16[496,512]{1,0:T(8,128)(2,1)S(1)} %get-tuple-element.79), channel_id=1, source_target_pairs={{0,480},{16,496},{32,0},{48,16},{64,32},{80,48},{96,64},{112,80},{... | collective-permute-start | bytes 1523720 | tf_op jit(solution)/shard_map/ppermute | solution.py:23
  40.2 28.9 %copy-start.12 = (bf16[496,512]{1,0:T(8,128)(2,1)}, bf16[496,512]{1,0:T(8,128)(2,1)S(1)}, u32[]{:S(2)}) copy-start(bf16[496,512]{1,0:T(8,128)(2,1)S(1)} %collective-permute-done.3) | copy-start | bytes 1523716
  41.4 27.7 %collective-permute-start.4 = (bf16[992,512]{1,0:T(8,128)(2,1)S(1)}, bf16[992,512]{1,0:T(8,128)(2,1)S(1)}, u32[]{:S(2)}, u32[]{:S(2)}) collective-permute-start(bf16[992,512]{1,0:T(8,128)(2,1)S(1)} %get-tuple-element.68), channel_id=1, source_target_pairs={{0,448},{16,464},{32,480},{48,496},{64,0},{80,16},{96,32},{112,48}... | collective-permute-start | bytes 3047432 | tf_op jit(solution)/shard_map/ppermute | solution.py:23
  69.1 49.0 %copy-start.3 = (bf16[992,512]{1,0:T(8,128)(2,1)}, bf16[992,512]{1,0:T(8,128)(2,1)S(1)}, u32[]{:S(2)}) copy-start(bf16[992,512]{1,0:T(8,128)(2,1)S(1)} %collective-permute-done.4) | copy-start | bytes 3047428
  70.8 61.9 %copy-start.123 = (f32[2]{0:T(128)S(1)}, f32[2]{0:T(128)}, u32[]{:S(2)}) copy-start(f32[2]{0:T(128)} %param.13) | copy-start | bytes 28
  70.8 62.4 %copy-start.133 = (s32[2]{0:T(128)S(1)}, s32[2]{0:T(128)}, u32[]{:S(2)}) copy-start(s32[2]{0:T(128)} %param.12) | copy-start | bytes 28
  70.8 62.6 %copy-start.132 = (s32[2,4]{1,0:T(2,128)S(1)}, s32[2,4]{1,0:T(2,128)}, u32[]{:S(2)}) copy-start(s32[2,4]{1,0:T(2,128)} %param.11) | copy-start | bytes 100
  70.8 64.3 %copy-start.74 = (bf16[256,256]{1,0:T(8,128)(2,1)S(1)}, bf16[256,256]{1,0:T(8,128)(2,1)}, u32[]{:S(2)}) copy-start(bf16[256,256]{1,0:T(8,128)(2,1)} %param.15) | copy-start | bytes 393220
  70.8 65.1 %copy-start = (bf16[256,256]{1,0:T(8,128)(2,1)S(1)}, bf16[256,256]{1,0:T(8,128)(2,1)}, u32[]{:S(2)}) copy-start(bf16[256,256]{1,0:T(8,128)(2,1)} %param.8) | copy-start | bytes 393220
  70.8 47.3 %collective-permute-start.5 = (bf16[1984,512]{1,0:T(8,128)(2,1)S(1)}, bf16[1984,512]{1,0:T(8,128)(2,1)S(1)}, u32[]{:S(2)}, u32[]{:S(2)}) collective-permute-start(bf16[1984,512]{1,0:T(8,128)(2,1)S(1)} %get-tuple-element.64), channel_id=1, source_target_pairs={{0,384},{16,400},{32,416},{48,432},{64,448},{80,464},{96,480},{112... | collective-permute-start | bytes 6094856 | tf_op jit(solution)/shard_map/ppermute | solution.py:23
  120.5 94.4 %collective-permute-start.6 = (bf16[3968,512]{1,0:T(8,128)(2,1)}, bf16[3968,512]{1,0:T(8,128)(2,1)}, u32[]{:S(2)}, u32[]{:S(2)}) collective-permute-start(bf16[3968,512]{1,0:T(8,128)(2,1)} %get-tuple-element.54), channel_id=1, source_target_pairs={{0,256},{16,272},{32,288},{48,304},{64,320},{80,336},{96,352},{112... | collective-permute-start | bytes 12189704 | tf_op jit(solution)/shard_map/ppermute | solution.py:23
  122.4 13.5 %collective-permute-start = (bf16[256,512]{1,0:T(8,128)(2,1)S(1)}, bf16[256,512]{1,0:T(8,128)(2,1)S(1)}, u32[]{:S(2)}, u32[]{:S(2)}) collective-permute-start(bf16[256,512]{1,0:T(8,128)(2,1)S(1)} %constant_dynamic-update-slice_fusion), channel_id=1, source_target_pairs={{0,16},{16,32},{32,48},{48,64},{64,80},{80,96},{96,112},{112,128},... | collective-permute-start | bytes 786440 | tf_op jit(solution)/shard_map/ppermute | solution.py:38
  126.9 9.0 %collective-permute-start.1 = (bf16[256,512]{1,0:T(8,128)(2,1)S(1)}, bf16[256,512]{1,0:T(8,128)(2,1)S(1)}, u32[]{:S(2)}, u32[]{:S(2)}) collective-permute-start(bf16[256,512]{1,0:T(8,128)(2,1)S(1)} %constant_dynamic-update-slice_fusion), channel_id=1, source_target_pairs={{16,0},{32,16},{48,32},{64,48},{80,64},{96,80},{112,96},{128,112},... | collective-permute-start | bytes 786440 | tf_op jit(solution)/shard_map/ppermute | solution.py:40
  141.5 73.4 %copy-start.6 = (bf16[2,4,128,128]{3,2,1,0:T(8,128)(2,1)}, bf16[2,4,128,128]{3,2,1,0:T(8,128)(2,1)S(1)}, u32[]{:S(2)}) copy-start(bf16[2,4,128,128]{3,2,1,0:T(8,128)(2,1)S(1)} %get-tuple-element.60) | copy-start | bytes 786436
  141.5 73.4 %copy-start.8 = (bf16[2,4,128,128]{3,2,1,0:T(8,128)(2,1)}, bf16[2,4,128,128]{3,2,1,0:T(8,128)(2,1)S(1)}, u32[]{:S(2)}) copy-start(bf16[2,4,128,128]{3,2,1,0:T(8,128)(2,1)S(1)} %get-tuple-element.61) | copy-start | bytes 786436
  214.9 8.4 %copy-start.13 = (bf16[496,512]{1,0:T(8,128)(2,1)S(1)}, bf16[496,512]{1,0:T(8,128)(2,1)}, u32[]{:S(2)}) copy-start(bf16[496,512]{1,0:T(8,128)(2,1)} %copy-done.12) | copy-start | bytes 1523716
  214.9 9.2 %copy-start.4 = (bf16[992,512]{1,0:T(8,128)(2,1)S(1)}, bf16[992,512]{1,0:T(8,128)(2,1)}, u32[]{:S(2)}) copy-start(bf16[992,512]{1,0:T(8,128)(2,1)} %copy-done.3) | copy-start | bytes 3047428
  237.6 70.7 %copy-start.19 = (bf16[2,128,512]{2,1,0:T(8,128)(2,1)}, bf16[2,128,512]{2,1,0:T(8,128)(2,1)S(1)}, u32[]{:S(2)}) copy-start(bf16[2,128,512]{2,1,0:T(8,128)(2,1)S(1)} %constant_dynamic-slice_fusion.3) | copy-start | bytes 786436
  238.2 67.8 %copy-start.20 = (bf16[4,64,512]{2,1,0:T(8,128)(2,1)}, bf16[4,64,512]{2,1,0:T(8,128)(2,1)S(1)}, u32[]{:S(2)}) copy-start(bf16[4,64,512]{2,1,0:T(8,128)(2,1)S(1)} %constant_dynamic-slice_fusion.2) | copy-start | bytes 786436
  238.5 13.5 %copy-start.51 = (f32[256,256]{0,1:T(8,128)}, f32[256,256]{0,1:T(8,128)S(1)}, u32[]{:S(2)}) copy-start(f32[256,256]{0,1:T(8,128)S(1)} %get-tuple-element.130) | copy-start | bytes 786436
  238.8 63.5 %copy-start.21 = (bf16[8,32,512]{2,1,0:T(8,128)(2,1)}, bf16[8,32,512]{2,1,0:T(8,128)(2,1)S(1)}, u32[]{:S(2)}) copy-start(bf16[8,32,512]{2,1,0:T(8,128)(2,1)S(1)} %constant_dynamic-slice_fusion.1) | copy-start | bytes 786436
  239.4 106.4 %copy-start.18 = (bf16[16,16,512]{2,1,0:T(8,128)(2,1)}, bf16[16,16,512]{2,1,0:T(8,128)(2,1)S(1)}, u32[]{:S(2)}) copy-start(bf16[16,16,512]{2,1,0:T(8,128)(2,1)S(1)} %constant_dynamic-slice_fusion) | copy-start | bytes 786436
  289.5 9.9 %copy-start.62 = (f32[256,256]{0,1:T(8,128)S(1)}, f32[256,256]{0,1:T(8,128)}, u32[]{:S(2)}) copy-start(f32[256,256]{0,1:T(8,128)} %copy-done.61) | copy-start | bytes 786436
  289.5 11.6 %copy-start.64 = (f32[256,256]{0,1:T(8,128)S(1)}, f32[256,256]{0,1:T(8,128)}, u32[]{:S(2)}) copy-start(f32[256,256]{0,1:T(8,128)} %copy-done.63) | copy-start | bytes 786436
  302.1 10.6 %copy-start.35 = (bf16[256,256]{0,1:T(8,128)(2,1)}, bf16[256,256]{0,1:T(8,128)(2,1)S(1)}, u32[]{:S(2)}) copy-start(bf16[256,256]{0,1:T(8,128)(2,1)S(1)} %fusion.50) | copy-start | bytes 393220
  302.3 12.0 %copy-start.34 = (bf16[256,256]{0,1:T(8,128)(2,1)}, bf16[256,256]{0,1:T(8,128)(2,1)S(1)}, u32[]{:S(2)}) copy-start(bf16[256,256]{0,1:T(8,128)(2,1)S(1)} %fusion.51) | copy-start | bytes 393220
  302.6 10.9 %copy-start.33 = (bf16[256,256]{0,1:T(8,128)(2,1)}, bf16[256,256]{0,1:T(8,128)(2,1)S(1)}, u32[]{:S(2)}) copy-start(bf16[256,256]{0,1:T(8,128)(2,1)S(1)} %fusion.55) | copy-start | bytes 393220
  302.9 12.3 %copy-start.30 = (bf16[256,256]{0,1:T(8,128)(2,1)}, bf16[256,256]{0,1:T(8,128)(2,1)S(1)}, u32[]{:S(2)}) copy-start(bf16[256,256]{0,1:T(8,128)(2,1)S(1)} %fusion.56) | copy-start | bytes 393220
  303.7 12.3 %copy-start.31 = (bf16[256,256]{0,1:T(8,128)(2,1)}, bf16[256,256]{0,1:T(8,128)(2,1)S(1)}, u32[]{:S(2)}) copy-start(bf16[256,256]{0,1:T(8,128)(2,1)S(1)} %fusion.52) | copy-start | bytes 393220
  304.0 12.2 %copy-start.29 = (bf16[256,256]{0,1:T(8,128)(2,1)}, bf16[256,256]{0,1:T(8,128)(2,1)S(1)}, u32[]{:S(2)}) copy-start(bf16[256,256]{0,1:T(8,128)(2,1)S(1)} %fusion.57) | copy-start | bytes 393220
  306.1 13.0 %copy-start.37 = (bf16[256,256]{0,1:T(8,128)(2,1)}, bf16[256,256]{0,1:T(8,128)(2,1)S(1)}, u32[]{:S(2)}) copy-start(bf16[256,256]{0,1:T(8,128)(2,1)S(1)} %fusion.49) | copy-start | bytes 393220
  306.3 13.5 %copy-start.36 = (bf16[256,256]{0,1:T(8,128)(2,1)}, bf16[256,256]{0,1:T(8,128)(2,1)S(1)}, u32[]{:S(2)}) copy-start(bf16[256,256]{0,1:T(8,128)(2,1)S(1)} %fusion.54) | copy-start | bytes 393220
  308.4 12.3 %copy-start.39 = (bf16[256,256]{0,1:T(8,128)(2,1)}, bf16[256,256]{0,1:T(8,128)(2,1)S(1)}, u32[]{:S(2)}) copy-start(bf16[256,256]{0,1:T(8,128)(2,1)S(1)} %fusion.48) | copy-start | bytes 393220
  308.6 12.9 %copy-start.38 = (bf16[256,256]{0,1:T(8,128)(2,1)}, bf16[256,256]{0,1:T(8,128)(2,1)S(1)}, u32[]{:S(2)}) copy-start(bf16[256,256]{0,1:T(8,128)(2,1)S(1)} %fusion.53) | copy-start | bytes 393220
  317.1 35.5 %collective-permute-start.9 = (bf16[128,512]{1,0:T(8,128)(2,1)}, bf16[128,512]{1,0:T(8,128)(2,1)}, u32[]{:S(2)}, u32[]{:S(2)}) collective-permute-start(bf16[128,512]{1,0:T(8,128)(2,1)} %select_convert_fusion), channel_id=1, source_target_pairs={{0,256},{16,272},{32,288},{48,304},{64,320},{80,336},{96,352},{112... | collective-permute-start | bytes 393224 | tf_op jit(solution)/shard_map/ppermute | solution.py:64
  324.2 18.2 %copy-start.28 = (f32[2,128,128]{2,1,0:T(8,128)S(1)}, f32[2,128,128]{2,1,0:T(8,128)}, u32[]{:S(2)}) copy-start(f32[2,128,128]{2,1,0:T(8,128)} %fusion.284) | copy-start | bytes 393220
  328.3 24.0 %copy-start.40 = (f32[256,128]{1,0:T(8,128)S(1)}, f32[256,128]{1,0:T(8,128)}, u32[]{:S(2)}) copy-start(f32[256,128]{1,0:T(8,128)} %convolution_multiply_fusion.17) | copy-start | bytes 393220
  328.3 24.0 %copy-start.41 = (f32[256,128]{1,0:T(8,128)S(1)}, f32[256,128]{1,0:T(8,128)}, u32[]{:S(2)}) copy-start(f32[256,128]{1,0:T(8,128)} %convolution_multiply_fusion.16) | copy-start | bytes 393220
  328.3 66.2 %collective-permute-start.7 = (bf16[256,512]{1,0:T(8,128)(2,1)}, bf16[256,512]{1,0:T(8,128)(2,1)}, u32[]{:S(2)}, u32[]{:S(2)}) collective-permute-start(bf16[256,512]{1,0:T(8,128)(2,1)} %convert_element_type.240), channel_id=1, source_target_pairs={{16,0},{32,16},{48,32},{64,48},{80,64},{96,80},{112,96},{128,112},... | collective-permute-start | bytes 786440 | tf_op jit(solution)/shard_map/ppermute | solution.py:50
  340.3 12.1 %copy-start.75 = (f32[256,128]{1,0:T(8,128)S(1)}, f32[256,128]{1,0:T(8,128)}, u32[]{:S(2)}) copy-start(f32[256,128]{1,0:T(8,128)} %fusion.124) | copy-start | bytes 393220
  340.3 12.1 %copy-start.76 = (f32[256,128]{1,0:T(8,128)S(1)}, f32[256,128]{1,0:T(8,128)}, u32[]{:S(2)}) copy-start(f32[256,128]{1,0:T(8,128)} %fusion.109) | copy-start | bytes 393220
  340.3 12.2 %copy-start.44 = (f32[256,128]{1,0:T(8,128)S(1)}, f32[256,128]{1,0:T(8,128)}, u32[]{:S(2)}) copy-start(f32[256,128]{1,0:T(8,128)} %convolution_multiply_fusion.21) | copy-start | bytes 393220
  340.3 12.2 %copy-start.45 = (f32[256,128]{1,0:T(8,128)S(1)}, f32[256,128]{1,0:T(8,128)}, u32[]{:S(2)}) copy-start(f32[256,128]{1,0:T(8,128)} %convolution_multiply_fusion.20) | copy-start | bytes 393220
  340.3 12.2 %copy-start.77 = (f32[256,128]{1,0:T(8,128)S(1)}, f32[256,128]{1,0:T(8,128)}, u32[]{:S(2)}) copy-start(f32[256,128]{1,0:T(8,128)} %fusion.130) | copy-start | bytes 393220
  340.3 12.2 %copy-start.78 = (f32[256,128]{1,0:T(8,128)S(1)}, f32[256,128]{1,0:T(8,128)}, u32[]{:S(2)}) copy-start(f32[256,128]{1,0:T(8,128)} %fusion.115) | copy-start | bytes 393220
  340.3 12.2 %copy-start.42 = (f32[256,128]{1,0:T(8,128)S(1)}, f32[256,128]{1,0:T(8,128)}, u32[]{:S(2)}) copy-start(f32[256,128]{1,0:T(8,128)} %convolution_multiply_fusion.23) | copy-start | bytes 393220
  340.3 12.2 %copy-start.43 = (f32[256,128]{1,0:T(8,128)S(1)}, f32[256,128]{1,0:T(8,128)}, u32[]{:S(2)}) copy-start(f32[256,128]{1,0:T(8,128)} %convolution_multiply_fusion.22) | copy-start | bytes 393220
  340.3 12.2 %copy-start.79 = (f32[256,128]{1,0:T(8,128)S(1)}, f32[256,128]{1,0:T(8,128)}, u32[]{:S(2)}) copy-start(f32[256,128]{1,0:T(8,128)} %fusion.133) | copy-start | bytes 393220
  340.3 12.2 %copy-start.80 = (f32[256,128]{1,0:T(8,128)S(1)}, f32[256,128]{1,0:T(8,128)}, u32[]{:S(2)}) copy-start(f32[256,128]{1,0:T(8,128)} %fusion.118) | copy-start | bytes 393220
  340.3 54.2 %collective-permute-start.8 = (bf16[256,512]{1,0:T(8,128)(2,1)}, bf16[256,512]{1,0:T(8,128)(2,1)}, u32[]{:S(2)}, u32[]{:S(2)}) collective-permute-start(bf16[256,512]{1,0:T(8,128)(2,1)} %convert_element_type.242), channel_id=1, source_target_pairs={{0,16},{16,32},{32,48},{48,64},{64,80},{80,96},{96,112},{112,128},... | collective-permute-start | bytes 786440 | tf_op jit(solution)/shard_map/ppermute | solution.py:50
  352.6 25.4 %copy-start.5 = (f32[256,512]{1,0:T(8,128)}, f32[256,512]{1,0:T(8,128)S(1)}, u32[]{:S(2)}) copy-start(f32[256,512]{1,0:T(8,128)S(1)} %pad_maximum_fusion.3) | copy-start | bytes 1572868
  352.6 23.7 %copy-start.32 = (bf16[256,256]{0,1:T(8,128)(2,1)S(1)}, bf16[256,256]{0,1:T(8,128)(2,1)}, u32[]{:S(2)}) copy-start(bf16[256,256]{0,1:T(8,128)(2,1)} %copy-done.31) | copy-start | bytes 393220
  353.8 7.1 %collective-permute-start.10 = (bf16[192,512]{1,0:T(8,128)(2,1)S(1)}, bf16[192,512]{1,0:T(8,128)(2,1)S(1)}, u32[]{:S(2)}, u32[]{:S(2)}) collective-permute-start(bf16[192,512]{1,0:T(8,128)(2,1)S(1)} %pad_maximum_fusion.10), channel_id=1, source_target_pairs={{0,128},{16,144},{32,160},{48,176},{64,192},{80,208},{96,224},{112... | collective-permute-start | bytes 589832 | tf_op jit(solution)/shard_map/ppermute | solution.py:64
  361.1 11.1 %collective-permute-start.11 = (bf16[224,512]{1,0:T(8,128)(2,1)S(1)}, bf16[224,512]{1,0:T(8,128)(2,1)S(1)}, u32[]{:S(2)}, u32[]{:S(2)}) collective-permute-start(bf16[224,512]{1,0:T(8,128)(2,1)S(1)} %pad_maximum_fusion.9), channel_id=1, source_target_pairs={{0,64},{16,80},{32,96},{48,112},{64,0},{80,16},{96,32},{112,48},{1... | collective-permute-start | bytes 688136 | tf_op jit(solution)/shard_map/ppermute | solution.py:64
  372.3 10.5 %copy-start.17 = (f32[64,512]{1,0:T(8,128)}, f32[64,512]{1,0:T(8,128)S(1)}, u32[]{:S(2)}) copy-start(f32[64,512]{1,0:T(8,128)S(1)} %convert_add_fusion.5) | copy-start | bytes 393220
  373.1 8.6 %collective-permute-start.12 = (bf16[240,512]{1,0:T(8,128)(2,1)}, bf16[240,512]{1,0:T(8,128)(2,1)}, u32[]{:S(2)}, u32[]{:S(2)}) collective-permute-start(bf16[240,512]{1,0:T(8,128)(2,1)} %pad_maximum_fusion.8), channel_id=1, source_target_pairs={{0,32},{16,48},{32,0},{48,16},{64,96},{80,112},{96,64},{112,80},{1... | collective-permute-start | bytes 737288 | tf_op jit(solution)/shard_map/ppermute | solution.py:64
  378.3 14.6 %copy-start.70 = (bf16[256,128]{1,0:T(8,128)(2,1)S(1)}, bf16[256,128]{1,0:T(8,128)(2,1)}, u32[]{:S(2)}) copy-start(bf16[256,128]{1,0:T(8,128)(2,1)} %fusion.61) | copy-start | bytes 196612
  387.8 5.7 %collective-permute-start.13 = (bf16[248,512]{1,0:T(8,128)(2,1)}, bf16[248,512]{1,0:T(8,128)(2,1)S(1)}, u32[]{:S(2)}, u32[]{:S(2)}) collective-permute-start(bf16[248,512]{1,0:T(8,128)(2,1)} %constant_dynamic-update-slice_fusion.57), channel_id=1, source_target_pairs={{0,16},{16,0},{32,48},{48,32},{64,80},{80,64},{96,112},{112,96},{1... | collective-permute-start | bytes 761864 | tf_op jit(solution)/shard_map/ppermute | solution.py:64
  (85 other events, 318.4 us)
